TPU v7x, 512 devices: a whole 4x8x8 slice. The times are simulated.
512 devices in a mesh: narrow: 16 (over x, z_hi), wide: 32 (over y, z_lo, core).
Axes of the slice: x: 4, y: 8, z: 8 (z_hi: 4, z_lo: 2; z = z_hi * 2 + z_lo), core: 2. Of those that a mesh axis runs over, the one named last changes fastest.
Arguments:
- vertex: float32 [16, 32, 512, 128], P('narrow', 'wide'), may hold values from -2 to 2
- vertex_state: float32 [16, 32, 512], P('narrow', 'wide'), may hold values from 0.05 to 1
- context: float32 [16, 32, 512, 128], P('narrow', 'wide'), may hold values from -2 to 2
- context_state: float32 [16, 32, 512], P('narrow', 'wide'), may hold values from 0.05 to 1
- hub: float32 [32, 2048, 128], P('wide'), may hold values from -2 to 2
- hub_state: float32 [32, 2048], P('wide'), may hold values from 0.05 to 1
- edge_src: int32 [16, 32, 2, 1024], P('narrow', 'wide'), may hold values from 0 to 511
- edge_ctx: int32 [16, 32, 2, 1024], P('narrow', 'wide'), may hold values from 0 to 2559, as said below
- negatives: int32 [16, 32, 2, 2, 1024], P('narrow', 'wide'), may hold values from 0 to 511
- counts: int32 [16, 32, 2], P('narrow', 'wide'), may hold values from 128 to 1024, as said below
Outputs:
- vertex_out: float32 [16, 32, 512, 128], P('narrow', 'wide')
- vertex_state_out: float32 [16, 32, 512], P('narrow', 'wide')
- context_out: float32 [16, 32, 512, 128], P('narrow', 'wide')
- context_state_out: float32 [16, 32, 512], P('narrow', 'wide')
- hub_out: float32 [32, 2048, 128], P('wide')
- hub_state_out: float32 [32, 2048], P('wide')
Inputs may be any that keep to these rules, and one draw needn't show every extreme that they name: `edge_ctx`: A value below 512 names a row of the context block that the device holds in that stratum; 512 + h names row h of the hub table of the device's index along wide. `counts`: slots at or beyond the count are not live; some device has every slot live in some stratum.
All inputs are finite; a program needn't handle non-finite values.
Results may differ from a plain program's by a relative error of at most 0.0003.
Values sent between devices are 32-bit elements; how exact they have to be, the bound alone decides.
A program may use at most 64 MiB of HBM per device.

v0:
```python
import jax
import jax.numpy as jnp
from jax import lax
from jax.sharding import PartitionSpec as P

LEARN_RATE = 0.5
NEG_WEIGHT = 0.0625


def shifted(value, axis, steps):
    count = lax.axis_size(axis)
    pairs = [(source, (source + steps) % count) for source in range(count)]
    return lax.ppermute(value, axis, pairs)


def adagrad(table_rows, row_state, gradient):
    new_state = row_state + jnp.mean(gradient * gradient, axis=-1)
    return (table_rows - LEARN_RATE * gradient * lax.rsqrt(new_state)[..., None], new_state)


def negative_batch(inputs):
    group_vecs, sample_vecs, group_live = inputs
    scores = jnp.dot(group_vecs, sample_vecs.T, precision=lax.Precision.HIGHEST)
    weights = NEG_WEIGHT * jax.nn.sigmoid(scores) * group_live[:, None]
    pulled = jnp.dot(weights, sample_vecs, precision=lax.Precision.HIGHEST)
    sample_grad = jnp.dot(weights.T, group_vecs, precision=lax.Precision.HIGHEST)
    return (pulled, sample_grad)


def stratum(
    vertex_rows,
    vertex_sums,
    block,
    block_sums,
    hub_rows,
    sources,
    targets,
    negative_ids,
    live_count,
):
    edge_total = sources.shape[0]
    block_len = block.shape[0]
    table = jnp.concatenate([block, hub_rows], axis=0)
    src_vecs = vertex_rows[sources]
    tgt_vecs = table[targets]
    live = (jnp.arange(edge_total) < live_count).astype(vertex_rows.dtype)
    positive = jnp.sum(src_vecs * tgt_vecs, axis=1)
    pos_grad = (jax.nn.sigmoid(positive) - 1.0) * live
    batches = negative_ids.shape[0]
    grouped = src_vecs.reshape(batches, -1, src_vecs.shape[1])
    neg_vecs = block[negative_ids]
    pulled, neg_rows = lax.map(negative_batch, (grouped, neg_vecs, live.reshape(batches, -1)))
    src_grad = pos_grad[:, None] * tgt_vecs + pulled.reshape(edge_total, -1)
    vertex_grad = jnp.zeros_like(vertex_rows).at[sources].add(src_grad)
    table_grad = jnp.zeros_like(table).at[targets].add(pos_grad[:, None] * src_vecs)
    table_grad = table_grad.at[negative_ids.reshape(-1)].add(
        neg_rows.reshape(-1, neg_rows.shape[2])
    )
    new_vertex, new_vsums = adagrad(vertex_rows, vertex_sums, vertex_grad)
    new_block, new_bsums = adagrad(block, block_sums, table_grad[:block_len])
    return (new_vertex, new_vsums, new_block, new_bsums, table_grad[block_len:])


def hub_update(hub_rows, hub_sums, deltas):
    totals = lax.psum(deltas, "narrow")
    hub_rows, hub_sums = adagrad(hub_rows, hub_sums, totals[0])
    return (hub_rows, hub_sums)


def per_device(
    vertex,
    vertex_state,
    context,
    context_state,
    hub,
    hub_state,
    edge_src,
    edge_ctx,
    negatives,
    counts,
):
    vrows = vertex[0, 0]
    vsums = vertex_state[0, 0]
    block = context[0, 0]
    bsums = context_state[0, 0]
    hub_rows = hub[0]
    hub_sums = hub_state[0]
    vrows, vsums, block, bsums, delta_first = stratum(
        vrows,
        vsums,
        block,
        bsums,
        hub_rows,
        edge_src[0, 0, 0],
        edge_ctx[0, 0, 0],
        negatives[0, 0, 0],
        counts[0, 0, 0],
    )
    hub_mid, sums_mid = hub_update(hub_rows, hub_sums, delta_first[None])
    block, bsums = shifted((block, bsums), "wide", 1)
    vrows, vsums, block, bsums, delta_second = stratum(
        vrows,
        vsums,
        block,
        bsums,
        hub_rows,
        edge_src[0, 0, 1],
        edge_ctx[0, 0, 1],
        negatives[0, 0, 1],
        counts[0, 0, 1],
    )
    hub_end, sums_end = hub_update(hub_mid, sums_mid, delta_second[None])
    return (
        vrows[None, None],
        vsums[None, None],
        block[None, None],
        bsums[None, None],
        hub_end[None],
        sums_end[None],
    )


def solution(mesh):
    in_specs = (
        P("narrow", "wide", None, None),
        P("narrow", "wide", None),
        P("narrow", "wide", None, None),
        P("narrow", "wide", None),
        P("wide", None, None),
        P("wide", None),
        P("narrow", "wide", None, None),
        P("narrow", "wide", None, None),
        P("narrow", "wide", None, None, None),
        P("narrow", "wide", None),
    )
    out_specs = (
        P("narrow", "wide", None, None),
        P("narrow", "wide", None),
        P("narrow", "wide", None, None),
        P("narrow", "wide", None),
        P("wide", None, None),
        P("wide", None),
    )
    return jax.shard_map(
        per_device, mesh=mesh, in_specs=in_specs, out_specs=out_specs, check_vma=False
    )
```

profile of v0, /device:TPU:56, one launch (start us, length us, event | category | flops | bytes accessed | tf_op | source)
XLA Modules:
  0.0 333.0 jit_solution(5172822340629918288)
XLA Ops:
  12.3 3.8 %gather_fusion = f32[1024,128]{1,0:T(8,128)S(1)} fusion(f32[512,128]{1,0:T(8,128)} %bitcast.151, s32[1024]{0:T(1024)S(1)} %broadcast_clamp_fusion.3), kind=kCustom, calls=%fused_computation | custom fusion | bytes 1052672 | tf_op jit(solution)/shard_map/gather | solution.py:44
  16.1 5.5 %gather_fusion.2 = f32[2048,128]{1,0:T(8,128)S(1)} fusion(f32[512,128]{1,0:T(8,128)S(1)} %bitcast.149, s32[2048]{0:T(1024)S(1)} %bitcast_clamp_fusion.1), kind=kCustom, calls=%fused_computation.2 | custom fusion | bytes 2105344 | tf_op jit(solution)/shard_map/gather | solution.py:51
  23.5 16.8 %while.24 = (s32[]{:T(128)}, f32[2,512,128]{2,1,0:T(8,128)}, f32[2,1024,128]{2,1,0:T(8,128)}, f32[2,512,128]{2,1,0:T(8,128)S(1)}, f32[2,1024,128]{2,1,0:T(8,128)S(1)}, /*index=5*/f32[2,512]{1,0:T(2,128)S(1)}, s32[]{:T(128)}) while((s32[]{:T(128)}, f32[2,512,128]{2,1,0:T(8,128)}, f32[2,1024,128]{2,1,0:T(8,128)}, f32[2,512,128]{2,1,0:T(8,128)S(1)}, ...), condition=%wide.region_2.3_spmd, body=%wide.region_1.2_spmd.sunk | while | flops 2418016768 | bytes 21243080 | solution.py:52
  23.5 2.1 divide_multiply_fusion.4
  25.6 1.8 fusion.68
  27.5 3.4 %fusion.69 = f32[2,1024,128]{2,1,0:T(8,128)S(1)} fusion(f32[2,1024,128]{2,1,0:T(8,128)S(1)} %copy-done.5, s32[]{:T(128)S(6)} %copy.29, f32[512,1024]{1,0:T(8,128)S(1)} %divide_multiply_fusion.4, f32[2,512,128]{2,1,0:T(8,128)S(1)} %get-tuple-element.216), kind=kOutput, calls=%fused_computation.14.clone.1 | convolution fusion | flops 805306368 | bytes 2884608 | tf_op jit(solution)/shard_map/while/body/eval_jaxpr/dot_general | solution.py:26
  31.9 2.1 divide_multiply_fusion.4
  34.0 1.8 fusion.68
  35.8 3.4 %fusion.69 = f32[2,1024,128]{2,1,0:T(8,128)S(1)} fusion(f32[2,1024,128]{2,1,0:T(8,128)S(1)} %copy-done.5, s32[]{:T(128)S(6)} %copy.29, f32[512,1024]{1,0:T(8,128)S(1)} %divide_multiply_fusion.4, f32[2,512,128]{2,1,0:T(8,128)S(1)} %get-tuple-element.216), kind=kOutput, calls=%fused_computation.14.clone.1 | convolution fusion | flops 805306368 | bytes 2884608 | tf_op jit(solution)/shard_map/while/body/eval_jaxpr/dot_general | solution.py:26
  40.3 4.0 %gather_fusion.1 = f32[1024,128]{1,0:T(8,128)} fusion(f32[2560,128]{1,0:T(8,128)S(1)} %pad_maximum_fusion.1, s32[1024]{0:T(1024)S(1)} %broadcast_clamp_fusion.1), kind=kCustom, calls=%fused_computation.1 | custom fusion | bytes 1052672 | tf_op jit(solution)/shard_map/gather | solution.py:45
  46.2 6.9 %scatter_custom_fusion.1 = f32[2560,128]{1,0:T(8,128)S(1)} fusion(s32[1024]{0:T(1024)S(1)} %bitcast.182, f32[]{:T(128)} %constant.63.clone.1, f32[1024,128]{1,0:T(8,128)S(1)} %bitcast.157, f32[1024]{0:T(1024)S(1)} %add_select_fusion.1), kind=kCustom, calls=%fused_computation.55 | custom fusion | flops 262144 | bytes 1839108 | tf_op jit(solution)/shard_map/scatter-add | solution.py:55
  53.1 12.5 %scatter_fusion = f32[2560,128]{1,0:T(8,128)S(1)} fusion(f32[2560,128]{1,0:T(8,128)S(1)} %scatter_custom_fusion.1, s32[2048]{0:T(1024)S(1)} %bitcast.167, f32[2048,128]{1,0:T(8,128)} %bitcast.162), kind=kCustom, calls=%fused_computation.8 | custom fusion | flops 262144 | bytes 3153920 | tf_op jit(solution)/shard_map/scatter-add | solution.py:56
  66.7 1.9 collective-permute-start
  69.9 6.1 %scatter_custom_fusion = f32[512,128]{1,0:T(8,128)S(1)} fusion(s32[1024]{0:T(1024)S(1)} %bitcast.180, f32[1024,128]{1,0:T(8,128)S(1)} %bitcast_add_fusion.1, f32[]{:T(128)} %constant.63.clone.1), kind=kCustom, calls=%fused_computation.75 | custom fusion | flops 131072 | bytes 262148 | tf_op jit(solution)/shard_map/scatter-add | solution.py:54
  77.0 2.8 gather_fusion.3
  79.9 5.5 %gather_fusion.5 = f32[2048,128]{1,0:T(8,128)S(1)} fusion(f32[512,128]{1,0:T(8,128)S(1)} %collective-permute-done, s32[2048]{0:T(1024)S(1)} %bitcast_clamp_fusion), kind=kCustom, calls=%fused_computation.5 | custom fusion | bytes 2105344 | tf_op jit(solution)/shard_map/gather | solution.py:51
  87.2 16.8 %while.25 = (s32[]{:T(128)}, f32[2,512,128]{2,1,0:T(8,128)}, f32[2,1024,128]{2,1,0:T(8,128)}, f32[2,512,128]{2,1,0:T(8,128)S(1)}, f32[2,1024,128]{2,1,0:T(8,128)S(1)}, /*index=5*/f32[2,512]{1,0:T(2,128)S(1)}, s32[]{:T(128)}) while((s32[]{:T(128)}, f32[2,512,128]{2,1,0:T(8,128)}, f32[2,1024,128]{2,1,0:T(8,128)}, ...), condition=%wide.region_10.11_spmd, body=%wide.region_9.10_spmd.sunk | while | flops 2418016768 | bytes 21243080 | solution.py:52
  87.2 2.1 divide_multiply_fusion.5
  89.3 1.8 fusion.76
  91.2 3.4 %fusion.77 = f32[2,1024,128]{2,1,0:T(8,128)S(1)} fusion(f32[2,1024,128]{2,1,0:T(8,128)S(1)} %copy-done.7, s32[]{:T(128)S(6)} %copy.39, f32[512,1024]{1,0:T(8,128)S(1)} %divide_multiply_fusion.5, f32[2,512,128]{2,1,0:T(8,128)S(1)} %get-tuple-element.237), kind=kOutput, calls=%fused_computation.31.clone.1 | convolution fusion | flops 805306368 | bytes 2884608 | tf_op jit(solution)/shard_map/while/body/eval_jaxpr/dot_general | solution.py:26
  95.6 2.1 divide_multiply_fusion.5
  97.7 1.8 fusion.76
  99.6 3.4 %fusion.77 = f32[2,1024,128]{2,1,0:T(8,128)S(1)} fusion(f32[2,1024,128]{2,1,0:T(8,128)S(1)} %copy-done.7, s32[]{:T(128)S(6)} %copy.39, f32[512,1024]{1,0:T(8,128)S(1)} %divide_multiply_fusion.5, f32[2,512,128]{2,1,0:T(8,128)S(1)} %get-tuple-element.237), kind=kOutput, calls=%fused_computation.31.clone.1 | convolution fusion | flops 805306368 | bytes 2884608 | tf_op jit(solution)/shard_map/while/body/eval_jaxpr/dot_general | solution.py:26
  104.1 4.0 %gather_fusion.4 = f32[1024,128]{1,0:T(8,128)} fusion(f32[2560,128]{1,0:T(8,128)S(1)} %pad_maximum_fusion, s32[1024]{0:T(1024)S(1)} %broadcast_clamp_fusion), kind=kCustom, calls=%fused_computation.4 | custom fusion | bytes 1052672 | tf_op jit(solution)/shard_map/gather | solution.py:45
  110.0 6.9 %scatter_custom_fusion.4 = f32[2560,128]{1,0:T(8,128)S(1)} fusion(s32[1024]{0:T(1024)S(1)} %bitcast.178, f32[]{:T(128)} %constant.63.clone.1, f32[1024,128]{1,0:T(8,128)S(1)} %bitcast.154, f32[1024]{0:T(1024)S(1)} %add_select_fusion), kind=kCustom, calls=%fused_computation.53 | custom fusion | flops 262144 | bytes 1839108 | tf_op jit(solution)/shard_map/scatter-add | solution.py:55
  116.8 12.6 %scatter_fusion.1 = f32[2560,128]{1,0:T(8,128)S(1)} fusion(f32[2560,128]{1,0:T(8,128)S(1)} %scatter_custom_fusion.4, s32[2048]{0:T(1024)S(1)} %bitcast.166, f32[2048,128]{1,0:T(8,128)} %bitcast.163), kind=kCustom, calls=%fused_computation.11 | custom fusion | flops 262144 | bytes 3153920 | tf_op jit(solution)/shard_map/scatter-add | solution.py:56
  130.5 4.5 %collective-permute-start.1 = (f32[512]{0:T(512)S(1)}, f32[512]{0:T(512)S(1)}, u32[]{:S(2)}, u32[]{:S(2)}) collective-permute-start(f32[512]{0:T(512)S(1)} %get-tuple-element.105), channel_id=1, source_target_pairs={{0,1},{1,2},{2,3},{3,4},{4,5},{5,6},{6,7},{7,8},{8,9},{9,10},{10,1... | collective-permute-start | bytes 6152 | tf_op jit(solution)/shard_map/ppermute | solution.py:13
  135.0 2.0 bitcast_add_fusion
  137.0 6.5 %scatter_custom_fusion.3 = f32[512,128]{1,0:T(8,128)S(1)} fusion(s32[1024]{0:T(1024)S(1)} %bitcast.176, f32[1024,128]{1,0:T(8,128)} %bitcast_add_fusion, f32[]{:T(128)} %constant.63.clone.1), kind=kCustom, calls=%fused_computation.73 | custom fusion | flops 131072 | bytes 262656 | tf_op jit(solution)/shard_map/scatter-add | solution.py:54
  146.7 175.0 %all-reduce.3.cloned.1.call-done = (f32[1,2048,128]{2,1,0:T(8,128)}, f32[1,2048,128]{2,1,0:T(8,128)}) async-done(((f32[1,2048,128]{2,1,0:T(8,128)}, f32[1,2048,128]{2,1,0:T(8,128)}), (f32[1,2048,128]{2,1,0:T(8,128)}, f32[1,2048,128]{2,1,0:T(8,128)})) %all-reduce.3.cloned.1.call-update) | async-done | bytes 2097168 | tf_op jit(solution)/shard_map/psum | solution.py:65
  321.7 2.3 multiply_reduce_fusion
  324.1 1.5 multiply_subtract_fusion
  (107 shorter events, 24.9 us)
Async XLA Ops:
  7.2 314.5 %all-reduce.3.cloned.1.call-start = ((), (), s32[]{:S(2)}) async-start(), calls=%async_computation | async-start | bytes 4194304 | tf_op jit(solution)/shard_map/psum | solution.py:65
  12.3 3.8 %copy-start = (f32[1,1,512,128]{3,2,1,0:T(8,128)S(1)}, f32[1,1,512,128]{3,2,1,0:T(8,128)}, u32[]{:S(2)}) copy-start(f32[1,1,512,128]{3,2,1,0:T(8,128)} %param.16) | copy-start | bytes 786436
  23.5 16.8 %copy-start.2 = (f32[1,2048,128]{2,1,0:T(8,128)S(1)}, f32[1,2048,128]{2,1,0:T(8,128)}, u32[]{:S(2)}) copy-start(f32[1,2048,128]{2,1,0:T(8,128)} %param.18) | copy-start | bytes 3145732
  23.5 2.1 copy-start.11
  25.6 1.8 copy-start.5
  27.4 3.4 %copy-start.12 = (f32[2,512,128]{2,1,0:T(8,128)}, f32[2,512,128]{2,1,0:T(8,128)S(1)}, u32[]{:S(2)}) copy-start(f32[2,512,128]{2,1,0:T(8,128)S(1)} %fusion.68) | copy-start | bytes 1572868 | tf_op jit(solution)/shard_map/while
  30.9 1.0 copy-start.6
  31.9 2.1 copy-start.11
  34.0 1.8 copy-start.5
  35.8 3.4 %copy-start.12 = (f32[2,512,128]{2,1,0:T(8,128)}, f32[2,512,128]{2,1,0:T(8,128)S(1)}, u32[]{:S(2)}) copy-start(f32[2,512,128]{2,1,0:T(8,128)S(1)} %fusion.68) | copy-start | bytes 1572868 | tf_op jit(solution)/shard_map/while
  39.3 1.0 copy-start.6
  53.1 12.7 %copy-start.18 = (f32[1,1,512]{2,1,0:T(1,128)S(1)}, f32[1,1,512]{2,1,0:T(1,128)}, u32[]{:S(2)}) copy-start(f32[1,1,512]{2,1,0:T(1,128)} %param.17) | copy-start | bytes 6148
  65.8 3.9 %copy-start.3 = (f32[1024,128]{1,0:T(8,128)S(1)}, f32[1024,128]{1,0:T(8,128)}, u32[]{:S(2)}) copy-start(f32[1024,128]{1,0:T(8,128)} %gather_fusion.1) | copy-start | bytes 1572868
  65.8 3.9 %copy-start.13 = (f32[2,512,128]{2,1,0:T(8,128)S(1)}, f32[2,512,128]{2,1,0:T(8,128)}, u32[]{:S(2)}) copy-start(f32[2,512,128]{2,1,0:T(8,128)} %get-tuple-element.72) | copy-start | bytes 1572868
  66.7 13.2 %collective-permute-start = (f32[512,128]{1,0:T(8,128)}, f32[512,128]{1,0:T(8,128)S(1)}, u32[]{:S(2)}, u32[]{:S(2)}) collective-permute-start(f32[512,128]{1,0:T(8,128)} %multiply_subtract_fusion.1), channel_id=1, source_target_pairs={{0,1},{1,2},{2,3},{3,4},{4,5},{5,6},{6,7},{7,8},{8,9},{9,10},{10,1... | collective-permute-start | bytes 786440 | tf_op jit(solution)/shard_map/ppermute | solution.py:13
  69.7 6.5 %copy-start.17 = (f32[1,1,512]{2,1,0:T(1,128)S(1)}, f32[1,1,512]{2,1,0:T(1,128)}, u32[]{:S(2)}) copy-start(f32[1,1,512]{2,1,0:T(1,128)} %param.15) | copy-start | bytes 6148
  69.7 6.6 %copy-start.1 = (f32[1,1,512,128]{3,2,1,0:T(8,128)S(1)}, f32[1,1,512,128]{3,2,1,0:T(8,128)}, u32[]{:S(2)}) copy-start(f32[1,1,512,128]{3,2,1,0:T(8,128)} %param.14) | copy-start | bytes 786436
  87.2 2.1 copy-start.14
  89.3 1.8 copy-start.7
  91.2 3.4 %copy-start.15 = (f32[2,512,128]{2,1,0:T(8,128)}, f32[2,512,128]{2,1,0:T(8,128)S(1)}, u32[]{:S(2)}) copy-start(f32[2,512,128]{2,1,0:T(8,128)S(1)} %fusion.76) | copy-start | bytes 1572868 | tf_op jit(solution)/shard_map/while
  94.6 1.0 copy-start.8
  95.6 2.1 copy-start.14
  97.7 1.8 copy-start.7
  99.5 3.4 %copy-start.15 = (f32[2,512,128]{2,1,0:T(8,128)}, f32[2,512,128]{2,1,0:T(8,128)S(1)}, u32[]{:S(2)}) copy-start(f32[2,512,128]{2,1,0:T(8,128)S(1)} %fusion.76) | copy-start | bytes 1572868 | tf_op jit(solution)/shard_map/while
  103.0 1.0 copy-start.8
  130.4 4.5 %copy-start.4 = (f32[1024,128]{1,0:T(8,128)S(1)}, f32[1024,128]{1,0:T(8,128)}, u32[]{:S(2)}) copy-start(f32[1024,128]{1,0:T(8,128)} %gather_fusion.4) | copy-start | bytes 1572868
  130.5 13.9 %collective-permute-start.1 = (f32[512]{0:T(512)S(1)}, f32[512]{0:T(512)S(1)}, u32[]{:S(2)}, u32[]{:S(2)}) collective-permute-start(f32[512]{0:T(512)S(1)} %get-tuple-element.105), channel_id=1, source_target_pairs={{0,1},{1,2},{2,3},{3,4},{4,5},{5,6},{6,7},{7,8},{8,9},{9,10},{10,1... | collective-permute-start | bytes 6152 | tf_op jit(solution)/shard_map/ppermute | solution.py:13
  145.8 178.2 %copy-start.16 = (f32[1,2048]{1,0:T(1,128)S(1)}, f32[1,2048]{1,0:T(1,128)}, u32[]{:S(2)}) copy-start(f32[1,2048]{1,0:T(1,128)} %param.19) | copy-start | bytes 24580
  321.7 2.3 copy-start.9
  321.7 2.4 copy-start.10
Sparse Core Ops, SparseCore 0:
  130.6 191.0 all-reduce.2
where the time goes:
time: 335 us; the launch traced here: 333 us
  waiting for transfers between devices  175 us (52%)
  other arithmetic  70.1 us (21%)
  local copies, waits for them, and re-layouts  37.4 us (11%)
  matrix products  29.3 us (9%)
  between operations  14.4 us (4%)
  starting transfers between devices  6.46 us (2%)
    psum x1, waiting for transfers between devices, hub_update(): totals = lax.psum(deltas, 'narrow')  175 us
    scatter-add x2, other arithmetic, stratum(): table_grad.at[negative_ids.reshape(-1)]  25.1 us
    scatter-add x2, other arithmetic, stratum(): jnp.zeros_like(table).at[targets].add(pos_grad[:, None] * src_vecs)  13.7 us
    dot_general x4, matrix products, negative_batch(): jnp.dot(weights.T, group_vecs, precision=lax.Precision.HIGHEST)  13.7 us
    scatter-add x2, other arithmetic, stratum(): vertex_grad = jnp.zeros_like(vertex_rows).at[sources].add(src_grad)  12.6 us
    gather x2, local copies, waits for them, and re-layouts, stratum(): neg_vecs = block[negative_ids]  10.9 us
    dot_general x4, matrix products, negative_batch(): scores = jnp.dot(group_vecs, sample_vecs.T, precision=lax.Precision.HIGHEST)  8.34 us
    gather x2, local copies, waits for them, and re-layouts, stratum(): tgt_vecs = table[targets]  7.98 us
  transfers between devices with their start and end apart: 3, of which 1 were waited for; matrix products, arithmetic and copies ran while one was open for 7% of the time, Pallas kernels for 0%

commit v1 on v0

v1 whole, which is shorter than its diff:
```python
import jax
import jax.numpy as jnp
from jax import lax
from jax.experimental import pallas as pl
from jax.experimental.pallas import tpu as pltpu
from jax.sharding import PartitionSpec as P

LEARN_RATE = 0.5
NEG_WEIGHT = 0.0625
MESH = pl.DeviceIdType.MESH
F32 = jnp.float32
BF16 = jnp.bfloat16

D = 128
ROWS = 512
HUB = 2048
EDGES = 1024
BATCH = 512
RING = 4
ORDER = (2, 1, 3, 0)
BLOCK = 128
HALF = 64
PACK = BLOCK + 8


def split(x):
    hi = x.astype(BF16)
    lo = (x - hi.astype(F32)).astype(BF16)
    return hi, lo


def mm(a, b):
    return jnp.dot(a, b, preferred_element_type=F32)


def one_hot(index_row, rows):
    row = lax.broadcasted_iota(jnp.int32, (rows, index_row.shape[1]), 0)
    return jnp.where(row == index_row, 1.0, 0.0).astype(BF16)


def adagrad_block(rows, sums_row, grad):
    old = jnp.broadcast_to(sums_row, (BLOCK, D)).T
    mean = jnp.sum(grad * grad, axis=1, keepdims=True) * (1.0 / D)
    sums = old + mean
    return rows - LEARN_RATE * grad * lax.rsqrt(sums), sums.T[0:1]


def kernel(
    v_ref, vs_ref, c_ref, cs_ref, hub_ref, hs_ref, src_ref, ctx_ref, neg_ref, cnt_ref,
    vo_ref, vso_ref, co_ref, cso_ref, ho_ref, hso_ref,
    hub_t, v_t, c_t, oh_hub, oh_src, oh_blk, chub_t, u_t, u2_t, w2, u2, pos_t, hist, grad_c,
    delta, parts, held, rx, rz, v_mid, block_out, block_in, gathered,
    send_sem, recv_sem, local_sem,
):
    narrow = lax.axis_index("narrow")
    wide = lax.axis_index("wide")
    n_wide = lax.axis_size("wide")
    x = narrow // RING
    z = lax.rem(narrow, RING)

    def at(xx, zz):
        return {"narrow": lax.rem(xx, RING) * RING + lax.rem(zz, RING)}

    x_right, x_left = at(x + 1, z), at(x + 3, z)
    z_right, z_left = at(x, z + 1), at(x, z + 3)
    w_next = {"wide": lax.rem(wide + 1, n_wide)}
    w_prev = {"wide": lax.rem(wide + n_wide - 1, n_wide)}

    barrier = pltpu.get_barrier_semaphore()
    for other in (x_right, x_left, z_right, z_left, w_next, w_prev):
        pl.semaphore_signal(barrier, inc=1, device_id=other, device_id_type=MESH)

    started = []

    def send(src, dst, device):
        slot = len(started)
        copy = pltpu.make_async_remote_copy(
            src_ref=src,
            dst_ref=dst,
            send_sem=send_sem.at[slot],
            recv_sem=recv_sem.at[slot],
            device_id=device,
            device_id_type=MESH,
        )
        copy.start()
        started.append(copy)
        return copy

    def hub_base(zz, xx):
        return pl.multiple_of(
            lax.rem(zz, RING) * (RING * BLOCK) + lax.rem(xx, RING) * BLOCK, BLOCK
        )


    def prepare_hub():
        for part in range(RING):
            rows = pl.ds(part * ROWS, ROWS)
            hi, lo = split(hub_ref[rows, :].T)
            hub_t[0:D, rows] = hi
            hub_t[D : 2 * D, rows] = lo

    def gather_hub(s):
        def body(tile, carry):
            cols = pl.ds(pl.multiple_of(tile * 256, 256), 256)
            hot = one_hot(ctx_ref[s : s + 1, cols] - ROWS, HUB)
            oh_hub[s, :, cols] = hot
            got = mm(hub_t[...], hot)
            chub_t[:, cols] = got[0:D] + got[D : 2 * D]
            return carry

        lax.fori_loop(0, EDGES // 256, body, 0)

    def live_row(s):
        slot = lax.broadcasted_iota(jnp.int32, (1, EDGES), 1)
        return jnp.where(slot < cnt_ref[0, s], 1.0, 0.0)

    def positive(score, live):
        return (0.5 * jnp.tanh(0.5 * score) - 0.5) * live

    def put_rows(ref, value_t):
        for part in range(EDGES // 256):
            hi, lo = split(value_t[:, part * 256 : (part + 1) * 256].T)
            rows = pl.ds(part * 256, 256)
            ref[rows, 0:D] = hi
            ref[rows, D : 2 * D] = lo

    def gather_vertices(s, rows):
        oh_src[...] = one_hot(src_ref[s : s + 1, :], ROWS)
        hi, lo = split(rows.T)
        v_t[0:D, :] = hi
        v_t[D : 2 * D, :] = lo
        got = mm(v_t[...], oh_src[...])
        u2_t[...] = got.astype(BF16)
        u_t[...] = got[0:D] + got[D : 2 * D]

    def hub_gradient(s):
        u = u_t[...]
        score = jnp.sum(u * chub_t[...], axis=0, keepdims=True)
        put_rows(w2, u * positive(score, live_row(s)))

    def hub_piece(s, k):
        rows = pl.ds(hub_base(z + ORDER[k], 0), ROWS)
        got = mm(oh_hub[s, rows, :], w2[...])
        delta[s, rows, :] = got[:, 0:D] + got[:, D : 2 * D]

    def block_edges(s, block):
        live = live_row(s)
        hot = one_hot(ctx_ref[s : s + 1, :], ROWS)
        oh_blk[...] = hot
        hi, lo = split(block.T)
        c_t[0:D, :] = hi
        c_t[D : 2 * D, :] = lo
        got = mm(c_t[...], hot)
        c_all = chub_t[...] + got[0:D] + got[D : 2 * D]
        u = u_t[...]
        score = jnp.sum(u * c_all, axis=0, keepdims=True)
        p = positive(score, live)
        pos_t[...] = p * c_all
        put_rows(w2, u * p)
        put_rows(u2, u * live)
        got = mm(oh_blk[...], w2[...])
        grad_c[...] = got[:, 0:D] + got[:, D : 2 * D]

    def count_negatives(s):
        for b in range(EDGES // BATCH):
            hot = one_hot(neg_ref[s, b : b + 1, :], ROWS)
            hist[s, b] = mm(hot, jnp.ones((hot.shape[1], D), BF16))

    def batch(s, b, block):
        cols = pl.ds(b * BATCH, BATCH)
        hi, lo = split(0.5 * block)
        both = u2_t[:, cols]
        half_score = mm(jnp.concatenate([hi, hi], axis=1), both) + mm(lo, both[0:D])
        q_hi, q_lo = split(0.5 * jnp.tanh(half_score) + 0.5)
        weighted = (NEG_WEIGHT * hist[s, b]) * block
        m_hi, m_lo = split(weighted.T)
        pulled = mm(jnp.concatenate([m_hi, m_lo], axis=0), q_hi)
        pulled = pulled[0:D] + pulled[D : 2 * D] + mm(m_hi, q_lo)
        slot = lax.broadcasted_iota(jnp.int32, (1, BATCH), 1) + b * BATCH
        pos_t[:, cols] += pulled * jnp.where(slot < cnt_ref[0, s], 1.0, 0.0)
        u_rows = u2[cols, :]
        sums = mm(q_hi, u_rows)
        sums = sums[:, 0:D] + sums[:, D : 2 * D] + mm(q_lo, u_rows[:, 0:D])
        grad_c[...] += (NEG_WEIGHT * hist[s, b]) * sums

    def update_vertices(read, write):
        put_rows(w2, pos_t[...])
        got = mm(oh_src[...], w2[...])
        grad = got[:, 0:D] + got[:, D : 2 * D]
        for part in range(ROWS // BLOCK):
            rows = slice(part * BLOCK, (part + 1) * BLOCK)
            write(part, *adagrad_block(*read(part), grad[rows]))

    def update_block(read, write):
        for part in range(ROWS // BLOCK):
            rows = slice(part * BLOCK, (part + 1) * BLOCK)
            write(part, *adagrad_block(*read(part), grad_c[rows, :]))


    x_copies = {}
    z_copies = {}

    def x_first(s, k):
        here = z + ORDER[k]
        two, one, back = hub_base(here, x + 2), hub_base(here, x + 1), hub_base(here, x + 3)
        d = delta.at[s]
        x_copies[s, k] = [
            send(d.at[pl.ds(two, HALF)], rx.at[s, k, 0, 0], x_right),
            send(d.at[pl.ds(two + HALF, HALF)], rx.at[s, k, 1, 0], x_left),
            send(d.at[pl.ds(one + HALF, HALF)], rx.at[s, k, 0, 1], x_right),
            send(d.at[pl.ds(back, HALF)], rx.at[s, k, 1, 1], x_left),
        ]

    def x_second(s, k):
        here = z + ORDER[k]
        one, back = hub_base(here, x + 1), hub_base(here, x + 3)
        d = delta.at[s]
        copies = x_copies[s, k]
        rows = pl.ds(one, HALF)
        copies[0].wait_recv()
        delta[s, rows, :] += rx[s, k, 0, 0]
        copies.append(send(d.at[rows], rx.at[s, k, 0, 2], x_right))
        rows = pl.ds(back + HALF, HALF)
        copies[1].wait_recv()
        delta[s, rows, :] += rx[s, k, 1, 0]
        copies.append(send(d.at[rows], rx.at[s, k, 1, 2], x_left))

    def x_last(s, k):
        mine = hub_base(z + ORDER[k], x)
        copies = x_copies[s, k]
        for copy in copies[2:]:
            copy.wait_recv()
        first = delta[s, pl.ds(mine, HALF), :] + rx[s, k, 0, 2] + rx[s, k, 1, 1]
        second = delta[s, pl.ds(mine + HALF, HALF), :] + rx[s, k, 0, 1] + rx[s, k, 1, 2]
        parts[s, k, 0:HALF, :] = first
        parts[s, k, HALF:BLOCK, :] = second
        part = parts.at[s, k]
        low, high = part.at[pl.ds(0, HALF)], part.at[pl.ds(HALF, HALF)]
        if k == 0:
            z_copies[s] = {
                (0, 0): send(low, rz.at[s, 0, 0], z_right),
                (1, 0): send(high, rz.at[s, 1, 0], z_left),
            }
        elif k == 1:
            z_copies[s][0, 1] = send(high, rz.at[s, 0, 1], z_right)
        elif k == 2:
            z_copies[s][1, 1] = send(low, rz.at[s, 1, 1], z_left)

    def z_second(s):
        copies = z_copies[s]
        copies[0, 0].wait_recv()
        parts[s, 1, 0:HALF, :] += rz[s, 0, 0]
        copies[0, 2] = send(parts.at[s, 1].at[pl.ds(0, HALF)], rz.at[s, 0, 2], z_right)
        copies[1, 0].wait_recv()
        parts[s, 2, HALF:BLOCK, :] += rz[s, 1, 0]
        copies[1, 2] = send(parts.at[s, 2].at[pl.ds(HALF, HALF)], rz.at[s, 1, 2], z_left)

    def z_last(s):
        copies = z_copies[s]
        for key in ((0, 1), (1, 1), (0, 2), (1, 2)):
            copies[key].wait_recv()
        first = parts[s, 3, 0:HALF, :] + rz[s, 0, 2] + rz[s, 1, 1]
        second = parts[s, 3, HALF:BLOCK, :] + rz[s, 0, 1] + rz[s, 1, 2]
        return jnp.concatenate([first, second], axis=0)


    prepare_hub()
    gather_hub(0)
    gather_vertices(0, v_ref[...])
    hub_gradient(0)
    pl.semaphore_wait(barrier, 6)
    for k in range(RING):
        hub_piece(0, k)
        x_first(0, k)
    block_edges(0, c_ref[...])
    count_negatives(0)
    for b in range(EDGES // BATCH):
        batch(0, b, c_ref[...])
    for k in range(RING):
        x_second(0, k)

    def part_of(part):
        return pl.ds(part * BLOCK, BLOCK)

    def read_vertex(part):
        return v_ref[part_of(part), :], vs_ref[:, part_of(part)]

    def write_vertex_mid(part, rows, sums):
        v_mid[part_of(part), :] = rows
        vso_ref[:, part_of(part)] = sums

    def read_block(part):
        return c_ref[part_of(part), :], cs_ref[:, part_of(part)]

    def write_block_out(part, rows, sums):
        block_out[part_of(part), :] = rows
        block_out[ROWS + part : ROWS + part + 1, :] = sums

    update_block(read_block, write_block_out)
    for part in range(ROWS // BLOCK, 8):
        block_out[ROWS + part : ROWS + part + 1, :] = jnp.zeros((1, D), F32)
    shift = send(block_out, block_in, w_next)
    update_vertices(read_vertex, write_vertex_mid)


    gather_hub(1)
    gather_vertices(1, v_mid[...])
    hub_gradient(1)
    for k in range(RING):
        hub_piece(1, k)
        x_first(1, k)
        x_last(0, k)
    count_negatives(1)
    z_second(0)
    shift.wait_recv()
    block_edges(1, block_in[0:ROWS, :])
    for k in range(RING):
        x_second(1, k)
    own = hub_base(z, x)
    own_rows = hub_ref[pl.ds(own, BLOCK), :]
    mid_rows, mid_sums = adagrad_block(own_rows, hs_ref[:, pl.ds(own, BLOCK)], z_last(0))
    held[0:BLOCK, :] = mid_rows
    held[BLOCK : BLOCK + 1, :] = mid_sums
    for b in range(EDGES // BATCH):
        batch(1, b, block_in[0:ROWS, :])
        x_last(1, 2 * b)
        x_last(1, 2 * b + 1)
    z_second(1)

    def read_vertex_mid(part):
        return v_mid[part_of(part), :], vso_ref[:, part_of(part)]

    def write_vertex(part, rows, sums):
        vo_ref[part_of(part), :] = rows
        vso_ref[:, part_of(part)] = sums

    def read_block_in(part):
        return block_in[part_of(part), :], block_in[ROWS + part : ROWS + part + 1, :]

    def write_block(part, rows, sums):
        co_ref[part_of(part), :] = rows
        cso_ref[:, part_of(part)] = sums


    end_rows, end_sums = adagrad_block(
        held[0:BLOCK, :], held[BLOCK : BLOCK + 1, :], z_last(1)
    )

    def slot_of(zz, xx):
        return lax.rem(zz, RING) * RING + lax.rem(xx, RING)

    me = slot_of(z, x)
    gathered[me, 0:BLOCK, :] = end_rows
    gathered[me, BLOCK:PACK, :] = jnp.broadcast_to(end_sums, (8, D))

    def spread(slot, device, lo=0, n=PACK):
        block = gathered.at[slot].at[pl.ds(lo, n)]
        return send(block, block, device)

    stores = []

    def store(zz, xx):
        slot = slot_of(zz, xx)
        copy = pltpu.make_async_copy(
            gathered.at[slot].at[pl.ds(0, BLOCK)],
            ho_ref.at[pl.ds(hub_base(zz, xx), BLOCK)],
            local_sem.at[len(stores)],
        )
        copy.start()
        stores.append(copy)
        hso_ref[:, pl.ds(hub_base(zz, xx), BLOCK)] = gathered[slot, BLOCK : BLOCK + 1, :]

    z_r = spread(me, z_right)
    z_l = spread(me, z_left)
    direct = {0: (spread(me, x_right), spread(me, x_left))}
    store(z, x)
    update_vertices(read_vertex_mid, write_vertex)
    update_block(read_block_in, write_block)

    z_r.wait_recv()
    from_left = slot_of(z + 3, x)
    z_fr = spread(from_left, z_right, 0, HALF)
    direct[3] = (spread(from_left, x_right), spread(from_left, x_left))
    store(z + 3, x)
    z_l.wait_recv()
    from_right = slot_of(z + 1, x)
    z_fl = spread(from_right, z_left, HALF, PACK - HALF)
    direct[1] = (spread(from_right, x_right), spread(from_right, x_left))
    store(z + 1, x)

    forwards = {}

    def forward(dz):
        right, left = direct[dz]
        right.wait_recv()
        fr = spread(slot_of(z + dz, x + 3), x_right, 0, HALF)
        store(z + dz, x + 3)
        left.wait_recv()
        fl = spread(slot_of(z + dz, x + 1), x_left, HALF, PACK - HALF)
        store(z + dz, x + 1)
        forwards[dz] = (fr, fl)

    def finish(dz):
        fr, fl = forwards[dz]
        fr.wait_recv()
        fl.wait_recv()
        store(z + dz, x + 2)

    forward(0)
    z_fr.wait_recv()
    z_fl.wait_recv()
    far = slot_of(z + 2, x)
    direct[2] = (spread(far, x_right), spread(far, x_left))
    store(z + 2, x)
    for dz in (3, 1, 2):
        forward(dz)
    for dz in (0, 3, 1, 2):
        finish(dz)

    for copy in started:
        copy.wait_send()
    for copy in stores:
        copy.wait()


N_COPIES = 2 * 24 + 2 * 6 + 1 + 4 + 16


def per_device(
    vertex, vertex_state, context, context_state, hub, hub_state, edge_src, edge_ctx, negatives, counts
):
    vmem = pl.BlockSpec(memory_space=pltpu.VMEM)
    shapes = (
        jax.ShapeDtypeStruct((ROWS, D), F32),
        jax.ShapeDtypeStruct((1, ROWS), F32),
        jax.ShapeDtypeStruct((ROWS, D), F32),
        jax.ShapeDtypeStruct((1, ROWS), F32),
        jax.ShapeDtypeStruct((HUB, D), F32),
        jax.ShapeDtypeStruct((1, HUB), F32),
    )
    scratch = [
        pltpu.VMEM((2 * D, HUB), BF16),
        pltpu.VMEM((2 * D, ROWS), BF16),
        pltpu.VMEM((2 * D, ROWS), BF16),
        pltpu.VMEM((2, HUB, EDGES), BF16),
        pltpu.VMEM((ROWS, EDGES), BF16),
        pltpu.VMEM((ROWS, EDGES), BF16),
        pltpu.VMEM((D, EDGES), F32),
        pltpu.VMEM((D, EDGES), F32),
        pltpu.VMEM((2 * D, EDGES), BF16),
        pltpu.VMEM((EDGES, 2 * D), BF16),
        pltpu.VMEM((EDGES, 2 * D), BF16),
        pltpu.VMEM((D, EDGES), F32),
        pltpu.VMEM((2, 2, ROWS, D), F32),
        pltpu.VMEM((ROWS, D), F32),
        pltpu.VMEM((2, HUB, D), F32),
        pltpu.VMEM((2, RING, BLOCK, D), F32),
        pltpu.VMEM((PACK, D), F32),
        pltpu.VMEM((2, RING, 2, 3, HALF, D), F32),
        pltpu.VMEM((2, 2, 3, HALF, D), F32),
        pltpu.VMEM((ROWS, D), F32),
        pltpu.VMEM((ROWS + 8, D), F32),
        pltpu.VMEM((ROWS + 8, D), F32),
        pltpu.VMEM((RING * RING, PACK, D), F32),
        pltpu.SemaphoreType.DMA((N_COPIES,)),
        pltpu.SemaphoreType.DMA((N_COPIES,)),
        pltpu.SemaphoreType.DMA((RING * RING,)),
    ]
    out = pl.pallas_call(
        kernel,
        out_shape=shapes,
        in_specs=[vmem] * 9 + [pl.BlockSpec(memory_space=pltpu.SMEM)],
        out_specs=(vmem, vmem, vmem, vmem, pl.BlockSpec(memory_space=pl.ANY), vmem),
        scratch_shapes=scratch,
        compiler_params=pltpu.CompilerParams(
            collective_id=0, has_side_effects=True, vmem_limit_bytes=56 * 1024 * 1024
        ),
        name="skipgram_window",
    )(
        vertex[0, 0],
        vertex_state[0],
        context[0, 0],
        context_state[0],
        hub[0],
        hub_state,
        edge_src[0, 0],
        edge_ctx[0, 0],
        negatives[0, 0],
        counts[0],
    )
    return (
        out[0][None, None],
        out[1][None],
        out[2][None, None],
        out[3][None],
        out[4][None],
        out[5],
    )


def solution(mesh):
    narrow_wide = lambda n: P("narrow", "wide", *([None] * n))
    in_specs = (
        narrow_wide(2),
        narrow_wide(1),
        narrow_wide(2),
        narrow_wide(1),
        P("wide", None, None),
        P("wide", None),
        narrow_wide(2),
        narrow_wide(2),
        narrow_wide(3),
        narrow_wide(1),
    )
    out_specs = (
        narrow_wide(2),
        narrow_wide(1),
        narrow_wide(2),
        narrow_wide(1),
        P("wide", None, None),
        P("wide", None),
    )
    return jax.shard_map(
        per_device, mesh=mesh, in_specs=in_specs, out_specs=out_specs, check_vma=False
    )
```

time: 335 us -> 68.8 us (0.21)
  waiting for transfers between devices: 175 us -> 0 us
  other arithmetic: 70.1 us -> 0 us
  Pallas kernels: 0 us -> 61 us
  local copies, waits for them, and re-layouts: 37.4 us -> 6.84 us
  matrix products: 29.3 us -> 0 us
  between operations: 14.4 us -> 0.66 us
  starting transfers between devices: 6.46 us -> 0 us
    psum x1 -> x0, waiting for transfers between devices: 175 us -> none  [hub_update(): totals = lax.psum(deltas, 'narrow')]
    pallas_call x0 -> x1, Pallas kernels: none -> 61 us  [per_device(): pl.pallas_call(kernel, out_shape=shapes, in_specs=[vmem] * 9 + [pl.BlockS...]
    scatter-add x6 -> x0, other arithmetic: 51.4 us -> none  [the longest x2 25.1 us: stratum(): table_grad.at[negative_ids.reshape(-1)]]
    dot_general x12 -> x0, matrix products: 29.3 us -> none  [the longest x4 13.7 us: negative_batch(): jnp.dot(weights.T, group_vecs, precision=lax.Precision.HIGHEST)]
    gather x6 -> x0, local copies, waits for them, and re-layouts: 25.5 us -> none  [the longest x2 10.9 us: stratum(): neg_vecs = block[negative_ids]]
    ppermute x2 -> x0, starting transfers between devices: 6.42 us -> none  [shifted(): return lax.ppermute(value, axis, pairs)]
    unnamed x25 -> x12, local copies, waits for them, and re-layouts: 0.79 us -> 6.84 us
    reduce_sum x7 -> x0, other arithmetic: 5.38 us -> none  [the longest x5 2.88 us: adagrad(): new_state = row_state + jnp.mean(gradient * gradient, axis=-1)]
  transfers between devices with their start and end apart: 3 -> 0, of which waited for: 1 -> 0; matrix products, arithmetic and copies ran while one was open for 7% -> 0% of each run, Pallas kernels for 0% -> 0%
where the time goes in v1:
time: 68.8 us; the launch traced here: 68.5 us
  Pallas kernels  61 us (89%)
  local copies, waits for them, and re-layouts  6.84 us (10%)
    pallas_call x1, Pallas kernels, per_device(): pl.pallas_call(kernel, out_shape=shapes, in_specs=[vmem] * 9 + [pl.BlockS...  61 us
    unnamed x12, local copies, waits for them, and re-layouts  6.84 us

profile of v1, /device:TPU:56, one launch (start us, length us, event | category | flops | bytes accessed | tf_op | source)
XLA Modules:
  0.0 68.5 jit_solution(17089948977065722194)
XLA Ops:
  0.6 61.0 %skipgram_window.1 = (f32[512,128]{1,0:T(8,128)}, f32[1,512]{1,0:T(1,128)}, f32[512,128]{1,0:T(8,128)}, f32[1,512]{1,0:T(1,128)}, f32[2048,128]{1,0:T(8,128)}, /*index=5*/f32[1,2048]{1,0:T(1,128)}) custom-call(f32[512,128]{1,0:T(8,128)} %bitcast.18, f32[1,512]{1,0:T(1,128)} %bitcast.23, f32[512,128]{1,0:T(8,128)} %bitcast.19, f32[1,512]{1,0:T(1,128)} %bitcast.24, ...), custom_call_target="tpu_custom_call" | custom-call | tf_op jit(solution)/shard_map/skipgram_window/pallas_call | solution.py:469
  61.6 0.0 copy-start
  61.6 1.8 %copy.22 = f32[1,1,512,128]{3,2,1,0:T(8,128)} copy(f32[1,1,512,128]{3,2,1,0:T(8,128)} %bitcast.17) | data formatting | bytes 524288
  63.4 1.3 %copy.23 = f32[1,1,512]{2,1,0:T(1,128)} copy(f32[1,1,512]{2,1,0:T(1,128)} %bitcast.26) | data formatting | bytes 4096
  64.6 0.0 copy-start.2
  64.6 1.7 %copy.24 = f32[1,1,512,128]{3,2,1,0:T(8,128)} copy(f32[1,1,512,128]{3,2,1,0:T(8,128)} %bitcast.16) | data formatting | bytes 524288
  66.3 0.0 copy-done.2
  66.3 0.6 copy.25
  66.9 0.0 copy-done
  66.9 0.0 copy-start.1
  66.9 1.0 %copy.26 = f32[1,2048,128]{2,1,0:T(8,128)} copy(f32[1,2048,128]{2,1,0:T(8,128)S(1)} %bitcast.15) | data formatting | bytes 2097152
  67.9 0.0 copy-done.1
  67.9 0.6 copy.27
Async XLA Ops:
  61.6 5.3 %copy-start = (f32[2048,128]{1,0:T(8,128)S(1)}, f32[2048,128]{1,0:T(8,128)}, u32[]{:S(2)}) copy-start(f32[2048,128]{1,0:T(8,128)} %get-tuple-element.16) | copy-start | bytes 3145732
  64.6 1.7 %copy-start.2 = (f32[1,512]{1,0:T(1,128)S(1)}, f32[1,512]{1,0:T(1,128)}, u32[]{:S(2)}) copy-start(f32[1,512]{1,0:T(1,128)} %get-tuple-element.15) | copy-start | bytes 6148
  66.9 1.0 %copy-start.1 = (f32[1,2048]{1,0:T(1,128)S(1)}, f32[1,2048]{1,0:T(1,128)}, u32[]{:S(2)}) copy-start(f32[1,2048]{1,0:T(1,128)} %get-tuple-element.29) | copy-start | bytes 24580

commit v2 on v1

v2 whole, which is shorter than its diff:
```python
import jax
import jax.numpy as jnp
from jax import lax
from jax.experimental import pallas as pl
from jax.experimental.pallas import tpu as pltpu
from jax.sharding import PartitionSpec as P

LEARN_RATE = 0.5
NEG_WEIGHT = 0.0625
MESH = pl.DeviceIdType.MESH
F32 = jnp.float32
BF16 = jnp.bfloat16

D = 128
ROWS = 512
HUB = 2048
EDGES = 1024
BATCH = 512
RING = 4
ORDER = (2, 1, 3, 0)
BLOCK = 128
HALF = 64
FIRST = ((0, 0, 128, "x"),)
SECOND = (((1, 0, 64, "x"),), ((1, 64, 64, "x"),))
DIRECT = SECOND[0] + SECOND[1]
PACK = HALF + 8


def split(x):
    hi = x.astype(BF16)
    lo = (x - hi.astype(F32)).astype(BF16)
    return hi, lo


def mm(a, b):
    return jnp.dot(a, b, preferred_element_type=F32)


def one_hot(index_row, rows):
    row = lax.broadcasted_iota(jnp.int32, (rows, index_row.shape[1]), 0)
    return jnp.where(row == index_row, 1.0, 0.0).astype(BF16)


def adagrad_block(rows, sums_row, grad):
    old = jnp.broadcast_to(sums_row, (BLOCK, D)).T
    mean = jnp.sum(grad * grad, axis=1, keepdims=True) * (1.0 / D)
    sums = old + mean
    return rows - LEARN_RATE * grad * lax.rsqrt(sums), sums.T[0:1]


def kernel(
    v_ref, vs_ref, c_ref, cs_ref, hub_ref, hs_ref, src_ref, ctx_ref, neg_ref, cnt_ref,
    vo_ref, vso_ref, co_ref, cso_ref, gathered,
    hub_t, v_t, c_t, oh_hub, oh_src, oh_blk, chub_t, u_t, u2_t, w2, u2, pos_t, pu_t, live_u_t,
    q_parts, hist, grad_c, delta, parts, mid_rows, mid_sums, far, rx, rz, v_mid, block_out, block_in,
    send_sem, recv_sem,
):
    narrow = lax.axis_index("narrow")
    wide = lax.axis_index("wide")
    n_wide = lax.axis_size("wide")
    x = narrow // RING
    z = lax.rem(narrow, RING)

    def at(xx, zz):
        return {"narrow": lax.rem(xx, RING) * RING + lax.rem(zz, RING)}

    x_right, x_left = at(x + 1, z), at(x + 3, z)
    z_right, z_left = at(x, z + 1), at(x, z + 3)
    x_far, z_far = at(x + 2, z), at(x, z + 2)
    w_next = {"wide": lax.rem(wide + 1, n_wide)}
    w_prev = {"wide": lax.rem(wide + n_wide - 1, n_wide)}

    barrier = pltpu.get_barrier_semaphore()
    for other in (x_right, x_left, x_far, z_right, z_left, z_far, w_next, w_prev):
        pl.semaphore_signal(barrier, inc=1, device_id=other, device_id_type=MESH)

    started = []

    def send(src, dst, device):
        slot = len(started)
        copy = pltpu.make_async_remote_copy(
            src_ref=src,
            dst_ref=dst,
            send_sem=send_sem.at[slot],
            recv_sem=recv_sem.at[slot],
            device_id=device,
            device_id_type=MESH,
        )
        copy.start()
        started.append(copy)
        return copy

    def hub_base(zz, xx):
        return pl.multiple_of(
            lax.rem(zz, RING) * (RING * BLOCK) + lax.rem(xx, RING) * BLOCK, BLOCK
        )


    def prepare_hub():
        for part in range(RING):
            rows = pl.ds(part * ROWS, ROWS)
            hi, lo = split(hub_ref[rows, :].T)
            hub_t[0:D, rows] = hi
            hub_t[D : 2 * D, rows] = lo

    def gather_hub(s):
        def body(tile, carry):
            cols = pl.ds(pl.multiple_of(tile * 256, 256), 256)
            hot = one_hot(ctx_ref[s : s + 1, cols] - ROWS, HUB)
            oh_hub[s, :, cols] = hot
            got = mm(hub_t[...], hot)
            chub_t[:, cols] = got[0:D] + got[D : 2 * D]
            return carry

        lax.fori_loop(0, EDGES // 256, body, 0)

    def live_row(s):
        slot = lax.broadcasted_iota(jnp.int32, (1, EDGES), 1)
        return jnp.where(slot < cnt_ref[0, s], 1.0, 0.0)

    def positive(score, live):
        return (0.5 * jnp.tanh(0.5 * score) - 0.5) * live

    def put_rows(ref, value_t):
        for part in range(EDGES // 256):
            hi, lo = split(value_t[:, part * 256 : (part + 1) * 256].T)
            rows = pl.ds(part * 256, 256)
            ref[rows, 0:D] = hi
            ref[rows, D : 2 * D] = lo

    def gather_vertices(s, rows):
        oh_src[...] = one_hot(src_ref[s : s + 1, :], ROWS)
        hi, lo = split(rows.T)
        v_t[0:D, :] = hi
        v_t[D : 2 * D, :] = lo
        got = mm(v_t[...], oh_src[...])
        u2_t[...] = got.astype(BF16)
        u_t[...] = got[0:D] + got[D : 2 * D]

    def hub_gradient(s):
        u = u_t[...]
        score = jnp.sum(u * chub_t[...], axis=0, keepdims=True)
        put_rows(w2, u * positive(score, live_row(s)))

    def hub_piece(s, k):
        rows = pl.ds(hub_base(z + ORDER[k], 0), ROWS)
        got = mm(oh_hub[s, rows, :], w2[...])
        delta[s, rows, :] = got[:, 0:D] + got[:, D : 2 * D]

    def block_edges(s, block):
        live = live_row(s)
        oh_blk[...] = one_hot(ctx_ref[s : s + 1, :], ROWS)
        hi, lo = split(block.T)
        c_t[0:D, :] = hi
        c_t[D : 2 * D, :] = lo
        got = mm(c_t[...], oh_blk[...])
        c_all = chub_t[...] + got[0:D] + got[D : 2 * D]
        u = u_t[...]
        score = jnp.sum(u * c_all, axis=0, keepdims=True)
        p = positive(score, live)
        pos_t[...] = p * c_all
        pu_t[...] = u * p
        live_u_t[...] = u * live

    def count_negatives(s):
        for b in range(EDGES // BATCH):
            hot = one_hot(neg_ref[s, b : b + 1, :], ROWS)
            hist[s, b] = mm(hot, jnp.ones((hot.shape[1], D), BF16))

    def batch(s, b, block):
        cols = pl.ds(b * BATCH, BATCH)
        hi, lo = split(0.5 * block)
        both = u2_t[:, cols]
        half_score = mm(jnp.concatenate([hi, hi], axis=1), both) + mm(lo, both[0:D])
        q_hi, q_lo = split(0.5 * jnp.tanh(half_score) + 0.5)
        q_parts[0, :, cols] = q_hi
        q_parts[1, :, cols] = q_lo
        weighted = (NEG_WEIGHT * hist[s, b]) * block
        m_hi, m_lo = split(weighted.T)
        pulled = mm(jnp.concatenate([m_hi, m_lo], axis=0), q_hi)
        pulled = pulled[0:D] + pulled[D : 2 * D] + mm(m_hi, q_lo)
        slot = lax.broadcasted_iota(jnp.int32, (1, BATCH), 1) + b * BATCH
        pos_t[:, cols] += pulled * jnp.where(slot < cnt_ref[0, s], 1.0, 0.0)

    def block_gradient(s):
        put_rows(u2, pu_t[...])
        got = mm(oh_blk[...], u2[...])
        total = got[:, 0:D] + got[:, D : 2 * D]
        put_rows(u2, live_u_t[...])
        for b in range(EDGES // BATCH):
            cols = pl.ds(b * BATCH, BATCH)
            u_rows = u2[cols, :]
            got = mm(q_parts[0, :, cols], u_rows)
            got = got[:, 0:D] + got[:, D : 2 * D] + mm(q_parts[1, :, cols], u_rows[:, 0:D])
            total = total + (NEG_WEIGHT * hist[s, b]) * got
        grad_c[...] = total

    def update_vertices(read, write):
        put_rows(w2, pos_t[...])
        got = mm(oh_src[...], w2[...])
        grad = got[:, 0:D] + got[:, D : 2 * D]
        for part in range(ROWS // BLOCK):
            rows = slice(part * BLOCK, (part + 1) * BLOCK)
            write(part, *adagrad_block(*read(part), grad[rows]))

    def update_block(read, write):
        for part in range(ROWS // BLOCK):
            rows = slice(part * BLOCK, (part + 1) * BLOCK)
            write(part, *adagrad_block(*read(part), grad_c[rows, :]))


    ring_copies = {}
    cross_copies = {}

    def base_of(part, along, across):
        if part[3] == "x":
            return hub_base(z + across, x + along) + part[1]
        return hub_base(z + along, x + across) + part[1]

    def device_of(part, along, across):
        return at(x + along, z + across) if part[3] == "x" else at(x + across, z + along)

    def ring_first(part, k):
        s, lo, n, _ = part
        half = n // 2
        right, left = device_of(part, 1, 0), device_of(part, 3, 0)
        two, one, back = (base_of(part, d, ORDER[k]) for d in (2, 1, 3))
        d = delta.at[s]

        def land(way, kind):
            return rx.at[s, k, way, kind].at[pl.ds(lo // 2, half)]

        if k == 0 and part in DIRECT:
            ring_copies[part, k] = [
                send(d.at[pl.ds(two, n)], far.at[s, 0].at[pl.ds(lo, n)], device_of(part, 2, 0)),
                send(d.at[pl.ds(one, n)], far.at[s, 1].at[pl.ds(lo, n)], right),
                send(d.at[pl.ds(back, n)], far.at[s, 2].at[pl.ds(lo, n)], left),
            ]
            return
        ring_copies[part, k] = [
            send(d.at[pl.ds(two, half)], land(0, 0), right),
            send(d.at[pl.ds(two + half, half)], land(1, 0), left),
            send(d.at[pl.ds(one + half, half)], land(0, 1), right),
            send(d.at[pl.ds(back, half)], land(1, 1), left),
        ]

    def ring_second(part, k):
        if k == 0 and part in DIRECT:
            return
        s, lo, n, _ = part
        half = n // 2
        one, back = (base_of(part, d, ORDER[k]) for d in (1, 3))
        d = delta.at[s]
        got = pl.ds(lo // 2, half)
        copies = ring_copies[part, k]
        rows = pl.ds(one, half)
        copies[0].wait_recv()
        delta[s, rows, :] += rx[s, k, 0, 0, got, :]
        copies.append(send(d.at[rows], rx.at[s, k, 0, 2].at[got], device_of(part, 1, 0)))
        rows = pl.ds(back + half, half)
        copies[1].wait_recv()
        delta[s, rows, :] += rx[s, k, 1, 0, got, :]
        copies.append(send(d.at[rows], rx.at[s, k, 1, 2].at[got], device_of(part, 3, 0)))

    def ring_last(part, k):
        s, lo, n, _ = part
        half = n // 2
        mine = base_of(part, 0, ORDER[k])
        copies = ring_copies[part, k]
        whole = pl.ds(lo, n)
        if k == 0 and part in DIRECT:
            total = delta[s, pl.ds(mine, n), :]
            for way in (1, 2, 0):
                copies[way].wait_recv()
                total = total + far[s, way, whole, :]
            parts[s, k, whole, :] = total
        else:
            got = pl.ds(lo // 2, half)
            for copy in copies[2:]:
                copy.wait_recv()
            parts[s, k, pl.ds(lo, half), :] = (
                delta[s, pl.ds(mine, half), :] + rx[s, k, 0, 2, got, :] + rx[s, k, 1, 1, got, :]
            )
            parts[s, k, pl.ds(lo + half, half), :] = (
                delta[s, pl.ds(mine + half, half), :]
                + rx[s, k, 0, 1, got, :]
                + rx[s, k, 1, 2, got, :]
            )
        if ORDER[k]:
            cross_copies[part, k] = send(
                parts.at[s, k].at[whole], rz.at[s, k].at[whole], device_of(part, 0, ORDER[k])
            )

    def reduced(part):
        s, lo, n, _ = part
        whole = pl.ds(lo, n)
        total = parts[s, RING - 1, whole, :]
        for k in (1, 2, 0):
            cross_copies[part, k].wait_recv()
            total = total + rz[s, k, whole, :]
        return total

    def each(function, parts_, pieces=(0, 1, 2, 3)):
        for part in parts_:
            for k in pieces:
                function(part, k)


    def slot_of(zz, xx):
        return lax.rem(zz, RING) * RING + lax.rem(xx, RING)

    me = slot_of(z, x)
    gathers = {}

    def spread(h, slot, device, lo=0, n=PACK):
        block = gathered.at[slot, h].at[pl.ds(lo, n)]
        return send(block, block, device)

    def gather_first(h):
        rows = pl.ds(h * HALF, HALF)
        grad = jnp.concatenate([reduced(part) for part in SECOND[h]], axis=0)
        sums = mid_sums[rows, :] + jnp.sum(grad * grad, axis=1, keepdims=True) * (1.0 / D)
        gathered[me, h, 0:HALF, :] = mid_rows[rows, :] - LEARN_RATE * grad * lax.rsqrt(sums)
        none = jnp.zeros((HALF, D), F32)
        column = jnp.concatenate([sums, none] if h == 0 else [none, sums], axis=0)
        gathered[me, h, HALF:PACK, :] = column.T[0:8]
        z_l, z_r = spread(h, me, z_left), spread(h, me, z_right)
        z_two = spread(h, me, z_far)
        gathers[h] = {
            "z": (z_r, z_l, z_two),
            0: (spread(h, me, x_right), spread(h, me, x_left)),
            "last": [],
        }

    def gather_near(h):
        z_r, z_l, _ = gathers[h]["z"]
        for copy, dz in ((z_r, 3), (z_l, 1)):
            copy.wait_recv()
            slot = slot_of(z + dz, x)
            gathers[h][dz] = (spread(h, slot, x_right), spread(h, slot, x_left))

    def gather_far(h):
        gathers[h]["z"][2].wait_recv()
        slot = slot_of(z + 2, x)
        for device in (x_far, x_right, x_left):
            gathers[h]["last"].append(spread(h, slot, device))

    def forward(h, dz):
        right, left = gathers[h][dz]
        last = gathers[h]["last"]
        right.wait_recv()
        last.append(spread(h, slot_of(z + dz, x + 3), x_right, 0, HALF // 2))
        left.wait_recv()
        last.append(spread(h, slot_of(z + dz, x + 1), x_left, HALF // 2, PACK - HALF // 2))


    def part_of(part):
        return pl.ds(part * BLOCK, BLOCK)

    def read_vertex(part):
        return v_ref[part_of(part), :], vs_ref[:, part_of(part)]

    def write_vertex_mid(part, rows, sums):
        v_mid[part_of(part), :] = rows
        vso_ref[:, part_of(part)] = sums

    def read_block(part):
        return c_ref[part_of(part), :], cs_ref[:, part_of(part)]

    def write_block_out(part, rows, sums):
        block_out[part_of(part), :] = rows
        block_out[ROWS + part : ROWS + part + 1, :] = sums

    def read_vertex_mid(part):
        return v_mid[part_of(part), :], vso_ref[:, part_of(part)]

    def write_vertex(part, rows, sums):
        vo_ref[part_of(part), :] = rows
        vso_ref[:, part_of(part)] = sums

    def read_block_in(part):
        return block_in[part_of(part), :], block_in[ROWS + part : ROWS + part + 1, :]

    def write_block(part, rows, sums):
        co_ref[part_of(part), :] = rows
        cso_ref[:, part_of(part)] = sums

    prepare_hub()
    gather_hub(0)
    gather_vertices(0, v_ref[...])
    hub_gradient(0)
    pl.semaphore_wait(barrier, 8)
    for k in range(RING):
        hub_piece(0, k)
        each(ring_first, [p for p in FIRST if p[3] == "x"], [k])
    each(ring_first, [p for p in FIRST if p[3] == "z"])
    block_edges(0, c_ref[...])
    count_negatives(0)
    batch(0, 0, c_ref[...])
    each(ring_second, FIRST)
    batch(0, 1, c_ref[...])
    each(ring_last, FIRST, [0])
    update_vertices(read_vertex, write_vertex_mid)


    gather_hub(1)
    each(ring_last, FIRST, [1, 2, 3])
    gather_vertices(1, v_mid[...])
    hub_gradient(1)
    for k in range(RING):
        hub_piece(1, k)
        each(ring_first, [p for p in SECOND[0] if p[3] == "x"], [k])
    each(ring_first, [p for p in SECOND[0] if p[3] == "z"])
    each(ring_first, SECOND[1])

    block_gradient(0)
    update_block(read_block, write_block_out)
    for part in range(ROWS // BLOCK, 8):
        block_out[ROWS + part : ROWS + part + 1, :] = jnp.zeros((1, D), F32)
    shift = send(block_out, block_in, w_next)
    count_negatives(1)
    each(ring_second, SECOND[0])
    each(ring_last, SECOND[0], [0])
    each(ring_second, SECOND[1])
    each(ring_last, SECOND[1], [0])
    own = pl.ds(hub_base(z, x), BLOCK)
    old = jnp.broadcast_to(hs_ref[:, own], (BLOCK, D)).T
    grad = jnp.concatenate([reduced(part) for part in FIRST], axis=0)
    sums = old + jnp.sum(grad * grad, axis=1, keepdims=True) * (1.0 / D)
    mid_sums[...] = sums
    mid_rows[...] = hub_ref[own, :] - LEARN_RATE * grad * lax.rsqrt(sums)
    shift.wait_recv()
    block_edges(1, block_in[0:ROWS, :])
    each(ring_last, SECOND[0], [1, 2, 3])
    batch(1, 0, block_in[0:ROWS, :])
    each(ring_last, SECOND[1], [1, 2, 3])
    batch(1, 1, block_in[0:ROWS, :])
    gather_first(0)
    update_vertices(read_vertex_mid, write_vertex)
    gather_first(1)
    block_gradient(1)
    update_block(read_block_in, write_block)
    gather_near(0)
    forward(0, 0)
    gather_far(0)
    gather_near(1)
    forward(0, 3)
    forward(0, 1)
    forward(1, 0)
    gather_far(1)
    forward(1, 3)
    forward(1, 1)
    for h in range(2):
        for copy in gathers[h]["last"]:
            copy.wait_recv()
    for copy in started:
        copy.wait_send()


def place(vo, vso, co, cso, rows, vo_ref, vso_ref, co_ref, cso_ref, ho_ref, hso_ref, sem):
    copies = [
        pltpu.make_async_copy(rows.at[:, :, pl.ds(0, HALF), :], ho_ref, sem.at[0]),
        pltpu.make_async_copy(vo, vo_ref, sem.at[1]),
        pltpu.make_async_copy(co, co_ref, sem.at[2]),
    ]
    for copy in copies:
        copy.start()
    vso_ref[...] = vso[...]
    cso_ref[...] = cso[...]
    for block in range(RING * RING):
        hso_ref[:, block * BLOCK : (block + 1) * BLOCK] = (
            rows[block, 0, HALF : HALF + 1, :] + rows[block, 1, HALF : HALF + 1, :]
        )
    for copy in copies:
        copy.wait()


PARTS = FIRST + SECOND[0] + SECOND[1]
N_COPIES = sum(27 - 3 * (p in DIRECT) for p in PARTS) + 1 + 2 * (3 + 3 * 4 + 3)


def per_device(
    vertex, vertex_state, context, context_state, hub, hub_state, edge_src, edge_ctx, negatives, counts
):
    vmem = pl.BlockSpec(memory_space=pltpu.VMEM)
    inner = (
        pltpu.VMEM((ROWS, D), F32),
        pltpu.VMEM((1, ROWS), F32),
        pltpu.VMEM((ROWS, D), F32),
        pltpu.VMEM((1, ROWS), F32),
        pltpu.VMEM((RING * RING, 2, PACK, D), F32),
    )
    shapes = (
        jax.ShapeDtypeStruct((ROWS, D), F32),
        jax.ShapeDtypeStruct((1, ROWS), F32),
        jax.ShapeDtypeStruct((ROWS, D), F32),
        jax.ShapeDtypeStruct((1, ROWS), F32),
        jax.ShapeDtypeStruct((RING * RING, 2, HALF, D), F32),
        jax.ShapeDtypeStruct((1, HUB), F32),
    )
    scratch = [
        pltpu.VMEM((2 * D, HUB), BF16),
        pltpu.VMEM((2 * D, ROWS), BF16),
        pltpu.VMEM((2 * D, ROWS), BF16),
        pltpu.VMEM((2, HUB, EDGES), BF16),
        pltpu.VMEM((ROWS, EDGES), BF16),
        pltpu.VMEM((ROWS, EDGES), BF16),
        pltpu.VMEM((D, EDGES), F32),
        pltpu.VMEM((D, EDGES), F32),
        pltpu.VMEM((2 * D, EDGES), BF16),
        pltpu.VMEM((EDGES, 2 * D), BF16),
        pltpu.VMEM((EDGES, 2 * D), BF16),
        pltpu.VMEM((D, EDGES), F32),
        pltpu.VMEM((D, EDGES), F32),
        pltpu.VMEM((D, EDGES), F32),
        pltpu.VMEM((2, ROWS, EDGES), BF16),
        pltpu.VMEM((2, 2, ROWS, D), F32),
        pltpu.VMEM((ROWS, D), F32),
        pltpu.VMEM((2, HUB, D), F32),
        pltpu.VMEM((2, RING, BLOCK, D), F32),
        pltpu.VMEM((BLOCK, D), F32),
        pltpu.VMEM((BLOCK, D), F32),
        pltpu.VMEM((2, 3, BLOCK, D), F32),
        pltpu.VMEM((2, RING, 2, 3, HALF, D), F32),
        pltpu.VMEM((2, RING - 1, BLOCK, D), F32),
        pltpu.VMEM((ROWS, D), F32),
        pltpu.VMEM((ROWS + 8, D), F32),
        pltpu.VMEM((ROWS + 8, D), F32),
        pltpu.SemaphoreType.DMA((N_COPIES,)),
        pltpu.SemaphoreType.DMA((N_COPIES,)),
    ]
    found = pl.pallas_call(
        kernel,
        out_shape=inner,
        in_specs=[vmem] * 9 + [pl.BlockSpec(memory_space=pltpu.SMEM)],
        out_specs=[vmem] * 5,
        scratch_shapes=scratch,
        compiler_params=pltpu.CompilerParams(
            collective_id=0, has_side_effects=True, vmem_limit_bytes=58 * 1024 * 1024
        ),
        name="skipgram_window",
    )(
        vertex[0, 0],
        vertex_state[0],
        context[0, 0],
        context_state[0],
        hub[0],
        hub_state,
        edge_src[0, 0],
        edge_ctx[0, 0],
        negatives[0, 0],
        counts[0],
    )
    hbm = pl.BlockSpec(memory_space=pl.ANY)
    out = pl.pallas_call(
        place,
        out_shape=shapes,
        in_specs=[vmem] * 5,
        out_specs=(hbm, vmem, hbm, vmem, hbm, vmem),
        scratch_shapes=[pltpu.SemaphoreType.DMA((3,))],
        compiler_params=pltpu.CompilerParams(vmem_limit_bytes=4 * 1024 * 1024),
        name="place_results",
    )(*found)
    return (
        out[0][None, None],
        out[1][None],
        out[2][None, None],
        out[3][None],
        out[4].reshape(1, HUB, D),
        out[5],
    )


def solution(mesh):
    narrow_wide = lambda n: P("narrow", "wide", *([None] * n))
    in_specs = (
        narrow_wide(2),
        narrow_wide(1),
        narrow_wide(2),
        narrow_wide(1),
        P("wide", None, None),
        P("wide", None),
        narrow_wide(2),
        narrow_wide(2),
        narrow_wide(3),
        narrow_wide(1),
    )
    out_specs = (
        narrow_wide(2),
        narrow_wide(1),
        narrow_wide(2),
        narrow_wide(1),
        P("wide", None, None),
        P("wide", None),
    )
    return jax.shard_map(
        per_device, mesh=mesh, in_specs=in_specs, out_specs=out_specs, check_vma=False
    )
```

time: 68.8 us -> 62.9 us (0.914)
  local copies, waits for them, and re-layouts: 6.84 us -> 0 us
    unnamed x12 -> x0, local copies, waits for them, and re-layouts: 6.84 us -> none
    pallas_call x1 -> x2, Pallas kernels: 61 us -> 61.6 us  [the longest x1 59.8 us: per_device(): pl.pallas_call(kernel, out_shape=inner, in_specs=[vmem] * 9 + [pl.BlockSp...]
where the time goes in v2:
time: 62.9 us; the launch traced here: 62.4 us
  Pallas kernels  61.6 us (98%)
  between operations  0.8 us (1%)
    pallas_call x1, Pallas kernels, per_device(): pl.pallas_call(kernel, out_shape=inner, in_specs=[vmem] * 9 + [pl.BlockSp...  59.8 us
    pallas_call x1, Pallas kernels, per_device(): pl.pallas_call(place, out_shape=shapes, in_specs=[vmem] * 5, out_specs=(h...  1.77 us

profile of v2, /device:TPU:56, one launch (start us, length us, event | category | flops | bytes accessed | tf_op | source)
XLA Modules:
  0.0 62.4 jit_solution(15357518844182436288)
XLA Ops:
  0.6 59.8 %skipgram_window.1 = (f32[512,128]{1,0:T(8,128)S(1)}, f32[1,512]{1,0:T(1,128)S(1)}, f32[512,128]{1,0:T(8,128)S(1)}, f32[1,512]{1,0:T(1,128)S(1)}, f32[16,2,72,128]{3,2,1,0:T(8,128)S(1)}) custom-call(f32[512,128]{1,0:T(8,128)} %bitcast.15, f32[1,512]{1,0:T(1,128)} %bitcast.20, f32[512,128]{1,0:T(8,128)} %bitcast.16, f32[1,512]{1,0:T(1,128)} %bitcast.21, ...), custom_call_target="tpu_custom_call" | custom-call | tf_op jit(solution)/shard_map/skipgram_window/pallas_call | solution.py:532
  60.5 1.8 %place_results.1 = (f32[512,128]{1,0:T(8,128)}, f32[1,512]{1,0:T(1,128)}, f32[512,128]{1,0:T(8,128)}, f32[1,512]{1,0:T(1,128)}, f32[16,2,64,128]{3,2,1,0:T(8,128)}, /*index=5*/f32[1,2048]{1,0:T(1,128)}) custom-call(f32[512,128]{1,0:T(8,128)S(1)} %get-tuple-element.17.vo, f32[1,512]{1,0:T(1,128)S(1)} %get-tuple-element.18.vso, ...), custom_call_target="tpu_custom_call" | custom-call | tf_op jit(solution)/shard_map/place_results/pallas_call | solution.py:555

commit v3 on v2

--- a/solution.py
+++ b/solution.py
@@ -37,8 +37,9 @@
 
 
 def one_hot(index_row, rows):
-    row = lax.broadcasted_iota(jnp.int32, (rows, index_row.shape[1]), 0)
-    return jnp.where(row == index_row, 1.0, 0.0).astype(BF16)
+    row = lax.broadcasted_iota(jnp.int16, (rows, index_row.shape[1]), 0)
+    one, none = jnp.ones((), BF16), jnp.zeros((), BF16)
+    return jnp.where(row == index_row.astype(jnp.int16), one, none)
 
 
 def adagrad_block(rows, sums_row, grad):
@@ -459,10 +460,15 @@
 
 def place(vo, vso, co, cso, rows, vo_ref, vso_ref, co_ref, cso_ref, ho_ref, hso_ref, sem):
     copies = [
-        pltpu.make_async_copy(rows.at[:, :, pl.ds(0, HALF), :], ho_ref, sem.at[0]),
-        pltpu.make_async_copy(vo, vo_ref, sem.at[1]),
-        pltpu.make_async_copy(co, co_ref, sem.at[2]),
+        pltpu.make_async_copy(
+            rows.at[pl.ds(i * RING, RING), :, pl.ds(0, HALF), :],
+            ho_ref.at[pl.ds(i * RING, RING)],
+            sem.at[i],
+        )
+        for i in range(RING)
     ]
+    copies.append(pltpu.make_async_copy(vo, vo_ref, sem.at[RING]))
+    copies.append(pltpu.make_async_copy(co, co_ref, sem.at[RING + 1]))
     for copy in copies:
         copy.start()
     vso_ref[...] = vso[...]
@@ -557,7 +563,7 @@
         out_shape=shapes,
         in_specs=[vmem] * 5,
         out_specs=(hbm, vmem, hbm, vmem, hbm, vmem),
-        scratch_shapes=[pltpu.SemaphoreType.DMA((3,))],
+        scratch_shapes=[pltpu.SemaphoreType.DMA((RING + 2,))],
         compiler_params=pltpu.CompilerParams(vmem_limit_bytes=4 * 1024 * 1024),
         name="place_results",
     )(*found)

time: 62.9 us -> 61.5 us (0.978)
  Pallas kernels: 61.6 us -> 60.5 us
    pallas_call x1, Pallas kernels: 59.8 us -> 58.7 us  [per_device(): pl.pallas_call(kernel, out_shape=inner, in_specs=[vmem] * 9 + [pl.BlockSp...]
where the time goes in v3:
time: 61.5 us; the launch traced here: 61.3 us
  Pallas kernels  60.5 us (98%)
  between operations  0.8 us (1%)
    pallas_call x1, Pallas kernels, per_device(): pl.pallas_call(kernel, out_shape=inner, in_specs=[vmem] * 9 + [pl.BlockSp...  58.7 us
    pallas_call x1, Pallas kernels, per_device(): pl.pallas_call(place, out_shape=shapes, in_specs=[vmem] * 5, out_specs=(h...  1.79 us

profile of v3, /device:TPU:56, one launch (start us, length us, event | category | flops | bytes accessed | tf_op | source)
XLA Modules:
  0.0 61.3 jit_solution(10759083166434682931)
XLA Ops:
  0.6 58.7 %skipgram_window.1 = (f32[512,128]{1,0:T(8,128)S(1)}, f32[1,512]{1,0:T(1,128)S(1)}, f32[512,128]{1,0:T(8,128)S(1)}, f32[1,512]{1,0:T(1,128)S(1)}, f32[16,2,72,128]{3,2,1,0:T(8,128)S(1)}) custom-call(f32[512,128]{1,0:T(8,128)} %bitcast.15, f32[1,512]{1,0:T(1,128)} %bitcast.20, f32[512,128]{1,0:T(8,128)} %bitcast.16, f32[1,512]{1,0:T(1,128)} %bitcast.21, ...), custom_call_target="tpu_custom_call" | custom-call | tf_op jit(solution)/shard_map/skipgram_window/pallas_call | solution.py:538
  59.4 1.8 %place_results.1 = (f32[512,128]{1,0:T(8,128)}, f32[1,512]{1,0:T(1,128)}, f32[512,128]{1,0:T(8,128)}, f32[1,512]{1,0:T(1,128)}, f32[16,2,64,128]{3,2,1,0:T(8,128)}, /*index=5*/f32[1,2048]{1,0:T(1,128)}) custom-call(f32[512,128]{1,0:T(8,128)S(1)} %get-tuple-element.17.vo, f32[1,512]{1,0:T(1,128)S(1)} %get-tuple-element.18.vso, ...), custom_call_target="tpu_custom_call" | custom-call | tf_op jit(solution)/shard_map/place_results/pallas_call | solution.py:561
